TPU v7x, 32 devices: a whole 2x2x4 slice. The times are simulated.
32 devices in a mesh: section: 4 (over x, core), blk: 8 (over z, y).
Axes of the slice: x: 2, y: 2, z: 4, core: 2. Of those that a mesh axis runs over, the one named last changes fastest.
Arguments:
- features: bfloat16 [4, 4096, 256], P(None, 'blk'), may hold values from -6 to 6
- tile_values: bfloat16 [4, 640, 128, 128], P(None, 'blk'), may hold values from -1 to 1
- tile_rows: int32 [4, 640], P(None, 'blk'), may hold values from 0 to 31, as said below
- tile_cols: int32 [4, 640], P(None, 'blk'), may hold values from 0 to 31, as said below
- tile_count: int32 [4, 8], P(None, 'blk'), may hold values from 10 to 80, as said below
- degrees: int32 [4, 4096], P(None, 'blk'), may hold values from 16 to 64
- self_weight: bfloat16 [4, 256, 256], P('section'), may hold values from -0.375 to 0.375
- neighbour_weight: bfloat16 [4, 256, 256], P('section'), may hold values from -0.375 to 0.375
Outputs:
- layer_outputs: bfloat16 [4, 4, 4096, 256], P('section', None, 'blk')
Inputs may be any that keep to these rules, and one draw needn't show every extreme that they name: `tile_rows`: slot k names a row block of its own blk index: between 4 * (k div 80) and 4 * (k div 80) + 3. `tile_cols`: slot k names a column block of a blk index at most 2 away from k div 80, counting around the axis; the 80 slots of one blk index name distinct row and column block pairs. `tile_count`: in every batch some blk index has all 80 slots live.
All inputs are finite; a program needn't handle non-finite values.
Results may differ from a plain program's by a relative error of at most 0.017.
Values may be sent and summed in bfloat16 or wider, within the bound.
A program may use at most 64 MiB of HBM per device.

v0:
```python
import jax
import jax.numpy as jnp
from jax import lax
from jax.sharding import PartitionSpec as P

REACH = 2


def from_behind(x, axis, by):
    peers = lax.axis_size(axis)
    return lax.ppermute(x, axis, [(i, (i + by) % peers) for i in range(peers)])


def shortened(x):

    def short(part):
        return part.astype(jnp.bfloat16) if part.dtype == jnp.float32 else part

    return jax.tree.map(short, x)


def passed_along(x, axis, by):
    peers = lax.axis_size(axis)
    pairs = [(i, i + by) for i in range(peers) if 0 <= i + by < peers]
    return lax.ppermute(x, axis, pairs)


def body(
    features, tile_values, tile_rows, tile_cols, tile_count, degrees, self_weight, neighbour_weight
):
    batch_total = features.shape[0]
    rows_dev = features.shape[1]
    feature_width = features.shape[2]
    block_size = tile_values.shape[2]
    slot_total = tile_values.shape[1]
    blocks_dev = rows_dev // block_size
    window_span = 2 * REACH + 1
    band_width = window_span * blocks_dev
    blk_count = lax.axis_size("blk")
    blk_index = lax.axis_index("blk")
    section_index = lax.axis_index("section")
    section_count = lax.axis_size("section")

    def gather_window(hidden):
        nearby = []
        for offset in (1, -1):
            nearby.append(from_behind(hidden, "blk", offset))
        distant = []
        for position, offset in enumerate((1, -1)):
            distant.append(from_behind(shortened(nearby[position]), "blk", offset))
        return jnp.concatenate([distant[0], nearby[0], hidden, nearby[1], distant[1]], axis=0)

    def aggregate(window, values, rows, cols, count):
        column_dev = cols // blocks_dev
        shifted = jnp.mod(column_dev - blk_index + REACH, blk_count)
        column_local = shifted * blocks_dev + jnp.mod(cols, blocks_dev)
        row_local = rows - blk_index * blocks_dev
        panels = window.reshape(band_width, block_size, feature_width)
        alive = jnp.arange(slot_total, dtype=jnp.int32) < count
        target = row_local * band_width + column_local
        placing = (
            (target[None, :] == jnp.arange(blocks_dev * band_width, dtype=jnp.int32)[:, None])
            & alive[None, :]
        ).astype(jnp.bfloat16)
        slab = jnp.dot(
            placing,
            values.reshape(slot_total, block_size * block_size),
            preferred_element_type=jnp.float32,
        ).astype(jnp.bfloat16)
        slab = slab.reshape(blocks_dev, band_width, block_size, block_size)
        summed = jnp.einsum("rcij,cjf->rif", slab, panels, preferred_element_type=jnp.float32)
        return summed.reshape(rows_dev, feature_width)

    def node_layer(hidden, batch, self_matrix, neighbour_matrix):
        values = lax.dynamic_index_in_dim(tile_values, batch, 0, keepdims=False)
        rows = lax.dynamic_index_in_dim(tile_rows, batch, 0, keepdims=False)
        cols = lax.dynamic_index_in_dim(tile_cols, batch, 0, keepdims=False)
        count = lax.dynamic_index_in_dim(tile_count, batch, 0, keepdims=False)[0]
        degree = lax.dynamic_index_in_dim(degrees, batch, 0, keepdims=False)
        window = gather_window(hidden)
        summed = aggregate(window, values, rows, cols, count)
        neighbour_mean = (summed / degree.astype(jnp.float32)[:, None]).astype(jnp.bfloat16)
        combined = jnp.dot(hidden, self_matrix, preferred_element_type=jnp.float32) + jnp.dot(
            neighbour_mean, neighbour_matrix, preferred_element_type=jnp.float32
        )
        active = jnp.maximum(combined, 0.0)
        scale = lax.rsqrt(jnp.mean(active * active, axis=-1, keepdims=True) + 1e-05)
        return (active * scale).astype(jnp.bfloat16)

    turn_total = batch_total + section_count - 1
    self_matrix = self_weight[0]
    neighbour_matrix = neighbour_weight[0]

    def advance(turn_index, state):
        incoming, stored = state
        batch = turn_index - section_index
        clamped = jnp.clip(batch, 0, batch_total - 1)
        valid = (batch >= 0) & (batch < batch_total)
        first_input = lax.dynamic_index_in_dim(features, clamped, 0, keepdims=False)
        hidden = jnp.where(section_index == 0, first_input, incoming)
        result = node_layer(hidden, clamped, self_matrix, neighbour_matrix)
        previous = lax.dynamic_index_in_dim(stored, clamped, 0, keepdims=False)
        stored = lax.dynamic_update_index_in_dim(
            stored, jnp.where(valid, result, previous), clamped, 0
        )
        incoming = passed_along(result, "section", 1)
        return (incoming, stored)

    incoming = jnp.zeros((rows_dev, feature_width), jnp.bfloat16)
    stored = jnp.zeros((batch_total, rows_dev, feature_width), jnp.bfloat16)
    incoming, stored = lax.fori_loop(0, turn_total, advance, (incoming, stored))
    return stored[None]


def solution(mesh):
    return jax.shard_map(
        body,
        mesh=mesh,
        in_specs=(
            P(None, "blk", None),
            P(None, "blk", None, None),
            P(None, "blk"),
            P(None, "blk"),
            P(None, "blk"),
            P(None, "blk"),
            P("section", None, None),
            P("section", None, None),
        ),
        out_specs=P("section", None, "blk", None),
        check_vma=False,
    )
```

profile of v0, /device:TPU:22, one launch (start us, length us, event | category | flops | bytes accessed | tf_op | source)
XLA Modules:
  0.0 320.3 jit_solution(10203038253133594339)
XLA Ops:
  1.0 318.4 %while.18 = (s32[]{:T(128)}, bf16[512,256]{0,1:T(8,128)(2,1)}, bf16[4,512,256]{2,1,0:T(8,128)(2,1)S(1)}, pred[]{:T(512)}, s32[]{:T(128)}, /*index=5*/bf16[4,512,...) while((s32[]{:T(128)}, bf16[512,256]{0,1:T(8,128)(2,1)}, ...), condition=%wide.region_2.3_spmd, body=%wide.region_0.2_spmd.sunk | while | flops 1017659904 | bytes 48512980 | solution.py:111
  5.3 2.1 constant_dynamic-slice_fusion.9
  9.4 2.0 fusion.47
  11.4 5.6 %collective-permute-done = bf16[512,256]{1,0:T(8,128)(2,1)} collective-permute-done((bf16[512,256]{1,0:T(8,128)(2,1)S(1)}, bf16[512,256]{1,0:T(8,128)(2,1)}, u32[]{:S(2)}, u32[]{:S(2)}) %collective-permute-start) | collective-permute-done | bytes 262176 | tf_op jit(solution)/shard_map/while/body/eval_jaxpr/ppermute | solution.py:11
  21.9 8.2 %collective-permute-done.1 = bf16[512,256]{1,0:T(8,128)(2,1)} collective-permute-done((bf16[512,256]{1,0:T(8,128)(2,1)}, bf16[512,256]{1,0:T(8,128)(2,1)}, u32[]{:S(2)}, u32[]{:S(2)}) %collective-permute-start.1) | collective-permute-done | bytes 262176 | tf_op jit(solution)/shard_map/while/body/eval_jaxpr/ppermute | solution.py:11
  36.6 3.3 %multiply_reduce_fusion.2 = (f32[512]{0:T(512)S(1)}, f32[512,256]{0,1:T(8,128)}) fusion(f32[512,256]{0,1:T(8,128)} %fusion.45, bf16[256,256]{1,0:T(8,128)(2,1)S(1)} %copy-done.4, bf16[512,20,128]{2,0,1:T(8,128)(2,1)S(1)} %bitcast.83, bf16[20,128,256]{2,1,0:T(8,128)(2,1)} %bitcast.79, f32[512]{0:T(512)S(1)} %bitcast.85), kind=kOutput, calls=%fused_computation.10.clone.1 | convolution fusion | flops 738983424 | bytes 5115904 | tf_op jit(solution)/shard_map/while/body/eval_jaxpr/dot_general | solution.py:83
  43.3 5.7 %collective-permute-done.4 = bf16[512,256]{0,1:T(8,128)(2,1)} collective-permute-done((bf16[512,256]{0,1:T(8,128)(2,1)S(1)}, bf16[512,256]{0,1:T(8,128)(2,1)}, u32[]{:S(2)}, u32[]{:S(2)}) %collective-permute-start.4) | collective-permute-done | bytes 262176 | tf_op jit(solution)/shard_map/while/body/eval_jaxpr/ppermute | solution.py:25
  51.3 2.0 collective-permute-start.2
  53.3 2.1 constant_dynamic-slice_fusion.9
  57.4 2.0 fusion.47
  59.4 6.5 %collective-permute-done = bf16[512,256]{1,0:T(8,128)(2,1)} collective-permute-done((bf16[512,256]{1,0:T(8,128)(2,1)S(1)}, bf16[512,256]{1,0:T(8,128)(2,1)}, u32[]{:S(2)}, u32[]{:S(2)}) %collective-permute-start) | collective-permute-done | bytes 262176 | tf_op jit(solution)/shard_map/while/body/eval_jaxpr/ppermute | solution.py:11
  68.8 2.0 collective-permute-start.3
  79.0 3.3 %multiply_reduce_fusion.2 = (f32[512]{0:T(512)S(1)}, f32[512,256]{0,1:T(8,128)}) fusion(f32[512,256]{0,1:T(8,128)} %fusion.45, bf16[256,256]{1,0:T(8,128)(2,1)S(1)} %copy-done.4, bf16[512,20,128]{2,0,1:T(8,128)(2,1)S(1)} %bitcast.83, bf16[20,128,256]{2,1,0:T(8,128)(2,1)} %bitcast.79, f32[512]{0:T(512)S(1)} %bitcast.85), kind=kOutput, calls=%fused_computation.10.clone.1 | convolution fusion | flops 738983424 | bytes 5115904 | tf_op jit(solution)/shard_map/while/body/eval_jaxpr/dot_general | solution.py:83
  85.7 6.5 %collective-permute-done.4 = bf16[512,256]{0,1:T(8,128)(2,1)} collective-permute-done((bf16[512,256]{0,1:T(8,128)(2,1)S(1)}, bf16[512,256]{0,1:T(8,128)(2,1)}, u32[]{:S(2)}, u32[]{:S(2)}) %collective-permute-start.4) | collective-permute-done | bytes 262176 | tf_op jit(solution)/shard_map/while/body/eval_jaxpr/ppermute | solution.py:25
  96.6 2.1 constant_dynamic-slice_fusion.9
  100.7 2.0 fusion.47
  102.7 2.7 collective-permute-done
  108.3 2.0 collective-permute-start.3
  118.7 3.3 %multiply_reduce_fusion.2 = (f32[512]{0:T(512)S(1)}, f32[512,256]{0,1:T(8,128)}) fusion(f32[512,256]{0,1:T(8,128)} %fusion.45, bf16[256,256]{1,0:T(8,128)(2,1)S(1)} %copy-done.4, bf16[512,20,128]{2,0,1:T(8,128)(2,1)S(1)} %bitcast.83, bf16[20,128,256]{2,1,0:T(8,128)(2,1)} %bitcast.79, f32[512]{0:T(512)S(1)} %bitcast.85), kind=kOutput, calls=%fused_computation.10.clone.1 | convolution fusion | flops 738983424 | bytes 5115904 | tf_op jit(solution)/shard_map/while/body/eval_jaxpr/dot_general | solution.py:83
  125.4 12.3 %collective-permute-done.4 = bf16[512,256]{0,1:T(8,128)(2,1)} collective-permute-done((bf16[512,256]{0,1:T(8,128)(2,1)S(1)}, bf16[512,256]{0,1:T(8,128)(2,1)}, u32[]{:S(2)}, u32[]{:S(2)}) %collective-permute-start.4) | collective-permute-done | bytes 262176 | tf_op jit(solution)/shard_map/while/body/eval_jaxpr/ppermute | solution.py:25
  140.0 2.0 collective-permute-start.2
  142.0 2.1 constant_dynamic-slice_fusion.9
  146.1 2.0 fusion.47
  148.1 4.0 %collective-permute-done = bf16[512,256]{1,0:T(8,128)(2,1)} collective-permute-done((bf16[512,256]{1,0:T(8,128)(2,1)S(1)}, bf16[512,256]{1,0:T(8,128)(2,1)}, u32[]{:S(2)}, u32[]{:S(2)}) %collective-permute-start) | collective-permute-done | bytes 262176 | tf_op jit(solution)/shard_map/while/body/eval_jaxpr/ppermute | solution.py:11
  154.9 2.0 collective-permute-start.3
  165.2 3.3 %multiply_reduce_fusion.2 = (f32[512]{0:T(512)S(1)}, f32[512,256]{0,1:T(8,128)}) fusion(f32[512,256]{0,1:T(8,128)} %fusion.45, bf16[256,256]{1,0:T(8,128)(2,1)S(1)} %copy-done.4, bf16[512,20,128]{2,0,1:T(8,128)(2,1)S(1)} %bitcast.83, bf16[20,128,256]{2,1,0:T(8,128)(2,1)} %bitcast.79, f32[512]{0:T(512)S(1)} %bitcast.85), kind=kOutput, calls=%fused_computation.10.clone.1 | convolution fusion | flops 738983424 | bytes 5115904 | tf_op jit(solution)/shard_map/while/body/eval_jaxpr/dot_general | solution.py:83
  171.9 11.2 %collective-permute-done.4 = bf16[512,256]{0,1:T(8,128)(2,1)} collective-permute-done((bf16[512,256]{0,1:T(8,128)(2,1)S(1)}, bf16[512,256]{0,1:T(8,128)(2,1)}, u32[]{:S(2)}, u32[]{:S(2)}) %collective-permute-start.4) | collective-permute-done | bytes 262176 | tf_op jit(solution)/shard_map/while/body/eval_jaxpr/ppermute | solution.py:25
  185.4 2.0 collective-permute-start.2
  187.4 2.1 constant_dynamic-slice_fusion.9
  191.5 2.0 fusion.47
  193.5 4.4 %collective-permute-done = bf16[512,256]{1,0:T(8,128)(2,1)} collective-permute-done((bf16[512,256]{1,0:T(8,128)(2,1)S(1)}, bf16[512,256]{1,0:T(8,128)(2,1)}, u32[]{:S(2)}, u32[]{:S(2)}) %collective-permute-start) | collective-permute-done | bytes 262176 | tf_op jit(solution)/shard_map/while/body/eval_jaxpr/ppermute | solution.py:11
  200.8 2.0 collective-permute-start.3
  211.1 3.3 %multiply_reduce_fusion.2 = (f32[512]{0:T(512)S(1)}, f32[512,256]{0,1:T(8,128)}) fusion(f32[512,256]{0,1:T(8,128)} %fusion.45, bf16[256,256]{1,0:T(8,128)(2,1)S(1)} %copy-done.4, bf16[512,20,128]{2,0,1:T(8,128)(2,1)S(1)} %bitcast.83, bf16[20,128,256]{2,1,0:T(8,128)(2,1)} %bitcast.79, f32[512]{0:T(512)S(1)} %bitcast.85), kind=kOutput, calls=%fused_computation.10.clone.1 | convolution fusion | flops 738983424 | bytes 5115904 | tf_op jit(solution)/shard_map/while/body/eval_jaxpr/dot_general | solution.py:83
  217.8 10.7 %collective-permute-done.4 = bf16[512,256]{0,1:T(8,128)(2,1)} collective-permute-done((bf16[512,256]{0,1:T(8,128)(2,1)S(1)}, bf16[512,256]{0,1:T(8,128)(2,1)}, u32[]{:S(2)}, u32[]{:S(2)}) %collective-permute-start.4) | collective-permute-done | bytes 262176 | tf_op jit(solution)/shard_map/while/body/eval_jaxpr/ppermute | solution.py:25
  230.8 2.0 collective-permute-start.2
  232.9 2.1 constant_dynamic-slice_fusion.9
  236.9 2.0 fusion.47
  239.0 4.9 %collective-permute-done = bf16[512,256]{1,0:T(8,128)(2,1)} collective-permute-done((bf16[512,256]{1,0:T(8,128)(2,1)S(1)}, bf16[512,256]{1,0:T(8,128)(2,1)}, u32[]{:S(2)}, u32[]{:S(2)}) %collective-permute-start) | collective-permute-done | bytes 262176 | tf_op jit(solution)/shard_map/while/body/eval_jaxpr/ppermute | solution.py:11
  246.7 2.0 collective-permute-start.3
  257.0 3.3 %multiply_reduce_fusion.2 = (f32[512]{0:T(512)S(1)}, f32[512,256]{0,1:T(8,128)}) fusion(f32[512,256]{0,1:T(8,128)} %fusion.45, bf16[256,256]{1,0:T(8,128)(2,1)S(1)} %copy-done.4, bf16[512,20,128]{2,0,1:T(8,128)(2,1)S(1)} %bitcast.83, bf16[20,128,256]{2,1,0:T(8,128)(2,1)} %bitcast.79, f32[512]{0:T(512)S(1)} %bitcast.85), kind=kOutput, calls=%fused_computation.10.clone.1 | convolution fusion | flops 738983424 | bytes 5115904 | tf_op jit(solution)/shard_map/while/body/eval_jaxpr/dot_general | solution.py:83
  263.7 10.3 %collective-permute-done.4 = bf16[512,256]{0,1:T(8,128)(2,1)} collective-permute-done((bf16[512,256]{0,1:T(8,128)(2,1)S(1)}, bf16[512,256]{0,1:T(8,128)(2,1)}, u32[]{:S(2)}, u32[]{:S(2)}) %collective-permute-start.4) | collective-permute-done | bytes 262176 | tf_op jit(solution)/shard_map/while/body/eval_jaxpr/ppermute | solution.py:25
  276.3 2.0 collective-permute-start.2
  278.3 2.1 constant_dynamic-slice_fusion.9
  282.3 2.0 fusion.47
  284.4 5.3 %collective-permute-done = bf16[512,256]{1,0:T(8,128)(2,1)} collective-permute-done((bf16[512,256]{1,0:T(8,128)(2,1)S(1)}, bf16[512,256]{1,0:T(8,128)(2,1)}, u32[]{:S(2)}, u32[]{:S(2)}) %collective-permute-start) | collective-permute-done | bytes 262176 | tf_op jit(solution)/shard_map/while/body/eval_jaxpr/ppermute | solution.py:11
  292.6 2.0 collective-permute-start.3
  302.9 3.3 %multiply_reduce_fusion.2 = (f32[512]{0:T(512)S(1)}, f32[512,256]{0,1:T(8,128)}) fusion(f32[512,256]{0,1:T(8,128)} %fusion.45, bf16[256,256]{1,0:T(8,128)(2,1)S(1)} %copy-done.4, bf16[512,20,128]{2,0,1:T(8,128)(2,1)S(1)} %bitcast.83, bf16[20,128,256]{2,1,0:T(8,128)(2,1)} %bitcast.79, f32[512]{0:T(512)S(1)} %bitcast.85), kind=kOutput, calls=%fused_computation.10.clone.1 | convolution fusion | flops 738983424 | bytes 5115904 | tf_op jit(solution)/shard_map/while/body/eval_jaxpr/dot_general | solution.py:83
  309.5 9.8 %collective-permute-done.4 = bf16[512,256]{0,1:T(8,128)(2,1)} collective-permute-done((bf16[512,256]{0,1:T(8,128)(2,1)S(1)}, bf16[512,256]{0,1:T(8,128)(2,1)}, u32[]{:S(2)}, u32[]{:S(2)}) %collective-permute-start.4) | collective-permute-done | bytes 262176 | tf_op jit(solution)/shard_map/while/body/eval_jaxpr/ppermute | solution.py:25
  (234 shorter events, 137.0 us)
Async XLA Ops:
  1.0 8.4 %copy-start = (bf16[4,512,256]{2,1,0:T(8,128)(2,1)}, bf16[4,512,256]{2,1,0:T(8,128)(2,1)S(1)}, u32[]{:S(2)}) copy-start(bf16[4,512,256]{2,1,0:T(8,128)(2,1)S(1)} %get-tuple-element.573) | copy-start | bytes 3145732 | tf_op jit(solution)/shard_map/while
  3.2 13.8 %collective-permute-start = (bf16[512,256]{1,0:T(8,128)(2,1)S(1)}, bf16[512,256]{1,0:T(8,128)(2,1)}, u32[]{:S(2)}, u32[]{:S(2)}) collective-permute-start(bf16[512,256]{1,0:T(8,128)(2,1)S(1)} %bitcast_select_fusion.3), channel_id=1, source_target_pairs={{0,1},{1,2},{2,3},{3,4},{4,5},{5,6},{6,7},{7,0},{8,9},{9,10},{10,1... | collective-permute-start | bytes 786440 | tf_op jit(solution)/shard_map/while/body/eval_jaxpr/ppermute | solution.py:11
  4.8 15.6 %collective-permute-start.2 = (bf16[512,256]{1,0:T(8,128)(2,1)S(1)}, bf16[512,256]{1,0:T(8,128)(2,1)}, u32[]{:S(2)}, u32[]{:S(2)}) collective-permute-start(bf16[512,256]{1,0:T(8,128)(2,1)S(1)} %bitcast_select_fusion.3), channel_id=1, source_target_pairs={{0,7},{1,0},{2,1},{3,2},{4,3},{5,4},{6,5},{7,6},{8,15},{9,8},{10,9... | collective-permute-start | bytes 786440 | tf_op jit(solution)/shard_map/while/body/eval_jaxpr/ppermute | solution.py:11
  17.0 13.1 %collective-permute-start.1 = (bf16[512,256]{1,0:T(8,128)(2,1)}, bf16[512,256]{1,0:T(8,128)(2,1)}, u32[]{:S(2)}, u32[]{:S(2)}) collective-permute-start(bf16[512,256]{1,0:T(8,128)(2,1)} %collective-permute-done), channel_id=1, source_target_pairs={{0,1},{1,2},{2,3},{3,4},{4,5},{5,6},{6,7},{7,0},{8,9},{9,10},{10,1... | collective-permute-start | bytes 786440 | tf_op jit(solution)/shard_map/while/body/eval_jaxpr/ppermute | solution.py:11
  20.3 16.3 %copy-start.4 = (bf16[256,256]{1,0:T(8,128)(2,1)S(1)}, bf16[256,256]{1,0:T(8,128)(2,1)}, u32[]{:S(2)}) copy-start(bf16[256,256]{1,0:T(8,128)(2,1)} %get-tuple-element.604) | copy-start | bytes 393220 | tf_op jit(solution)/shard_map/while
  20.3 15.5 %collective-permute-start.3 = (bf16[512,256]{1,0:T(8,128)(2,1)}, bf16[512,256]{1,0:T(8,128)(2,1)S(1)}, u32[]{:S(2)}, u32[]{:S(2)}) collective-permute-start(bf16[512,256]{1,0:T(8,128)(2,1)} %collective-permute-done.2), channel_id=1, source_target_pairs={{0,7},{1,0},{2,1},{3,2},{4,3},{5,4},{6,5},{7,6},{8,15},{9,8},{10,9... | collective-permute-start | bytes 786440 | tf_op jit(solution)/shard_map/while/body/eval_jaxpr/ppermute | solution.py:11
  41.2 7.8 %collective-permute-start.4 = (bf16[512,256]{0,1:T(8,128)(2,1)S(1)}, bf16[512,256]{0,1:T(8,128)(2,1)}, u32[]{:S(2)}, u32[]{:S(2)}) collective-permute-start(bf16[512,256]{0,1:T(8,128)(2,1)S(1)} %get-tuple-element.550), channel_id=1, source_target_pairs={{0,8},{8,16},{16,24},{1,9},{9,17},{17,25},{2,10},{10,18},{18,26},{... | collective-permute-start | bytes 786440 | tf_op jit(solution)/shard_map/while/body/eval_jaxpr/ppermute | solution.py:25
  49.0 8.4 %copy-start = (bf16[4,512,256]{2,1,0:T(8,128)(2,1)}, bf16[4,512,256]{2,1,0:T(8,128)(2,1)S(1)}, u32[]{:S(2)}) copy-start(bf16[4,512,256]{2,1,0:T(8,128)(2,1)S(1)} %get-tuple-element.573) | copy-start | bytes 3145732 | tf_op jit(solution)/shard_map/while
  51.2 14.7 %collective-permute-start = (bf16[512,256]{1,0:T(8,128)(2,1)S(1)}, bf16[512,256]{1,0:T(8,128)(2,1)}, u32[]{:S(2)}, u32[]{:S(2)}) collective-permute-start(bf16[512,256]{1,0:T(8,128)(2,1)S(1)} %bitcast_select_fusion.3), channel_id=1, source_target_pairs={{0,1},{1,2},{2,3},{3,4},{4,5},{5,6},{6,7},{7,0},{8,9},{9,10},{10,1... | collective-permute-start | bytes 786440 | tf_op jit(solution)/shard_map/while/body/eval_jaxpr/ppermute | solution.py:11
  51.3 17.5 %collective-permute-start.2 = (bf16[512,256]{1,0:T(8,128)(2,1)S(1)}, bf16[512,256]{1,0:T(8,128)(2,1)}, u32[]{:S(2)}, u32[]{:S(2)}) collective-permute-start(bf16[512,256]{1,0:T(8,128)(2,1)S(1)} %bitcast_select_fusion.3), channel_id=1, source_target_pairs={{0,7},{1,0},{2,1},{3,2},{4,3},{5,4},{6,5},{7,6},{8,15},{9,8},{10,9... | collective-permute-start | bytes 786440 | tf_op jit(solution)/shard_map/while/body/eval_jaxpr/ppermute | solution.py:11
  65.9 6.7 %collective-permute-start.1 = (bf16[512,256]{1,0:T(8,128)(2,1)}, bf16[512,256]{1,0:T(8,128)(2,1)}, u32[]{:S(2)}, u32[]{:S(2)}) collective-permute-start(bf16[512,256]{1,0:T(8,128)(2,1)} %collective-permute-done), channel_id=1, source_target_pairs={{0,1},{1,2},{2,3},{3,4},{4,5},{5,6},{6,7},{7,0},{8,9},{9,10},{10,1... | collective-permute-start | bytes 786440 | tf_op jit(solution)/shard_map/while/body/eval_jaxpr/ppermute | solution.py:11
  68.7 10.3 %copy-start.4 = (bf16[256,256]{1,0:T(8,128)(2,1)S(1)}, bf16[256,256]{1,0:T(8,128)(2,1)}, u32[]{:S(2)}) copy-start(bf16[256,256]{1,0:T(8,128)(2,1)} %get-tuple-element.604) | copy-start | bytes 393220 | tf_op jit(solution)/shard_map/while
  68.8 9.6 %collective-permute-start.3 = (bf16[512,256]{1,0:T(8,128)(2,1)}, bf16[512,256]{1,0:T(8,128)(2,1)S(1)}, u32[]{:S(2)}, u32[]{:S(2)}) collective-permute-start(bf16[512,256]{1,0:T(8,128)(2,1)} %collective-permute-done.2), channel_id=1, source_target_pairs={{0,7},{1,0},{2,1},{3,2},{4,3},{5,4},{6,5},{7,6},{8,15},{9,8},{10,9... | collective-permute-start | bytes 786440 | tf_op jit(solution)/shard_map/while/body/eval_jaxpr/ppermute | solution.py:11
  83.6 8.6 %collective-permute-start.4 = (bf16[512,256]{0,1:T(8,128)(2,1)S(1)}, bf16[512,256]{0,1:T(8,128)(2,1)}, u32[]{:S(2)}, u32[]{:S(2)}) collective-permute-start(bf16[512,256]{0,1:T(8,128)(2,1)S(1)} %get-tuple-element.550), channel_id=1, source_target_pairs={{0,8},{8,16},{16,24},{1,9},{9,17},{17,25},{2,10},{10,18},{18,26},{... | collective-permute-start | bytes 786440 | tf_op jit(solution)/shard_map/while/body/eval_jaxpr/ppermute | solution.py:25
  92.2 8.4 %copy-start = (bf16[4,512,256]{2,1,0:T(8,128)(2,1)}, bf16[4,512,256]{2,1,0:T(8,128)(2,1)S(1)}, u32[]{:S(2)}) copy-start(bf16[4,512,256]{2,1,0:T(8,128)(2,1)S(1)} %get-tuple-element.573) | copy-start | bytes 3145732 | tf_op jit(solution)/shard_map/while
  94.5 10.9 %collective-permute-start = (bf16[512,256]{1,0:T(8,128)(2,1)S(1)}, bf16[512,256]{1,0:T(8,128)(2,1)}, u32[]{:S(2)}, u32[]{:S(2)}) collective-permute-start(bf16[512,256]{1,0:T(8,128)(2,1)S(1)} %bitcast_select_fusion.3), channel_id=1, source_target_pairs={{0,1},{1,2},{2,3},{3,4},{4,5},{5,6},{6,7},{7,0},{8,9},{9,10},{10,1... | collective-permute-start | bytes 786440 | tf_op jit(solution)/shard_map/while/body/eval_jaxpr/ppermute | solution.py:11
  94.7 13.5 %collective-permute-start.2 = (bf16[512,256]{1,0:T(8,128)(2,1)S(1)}, bf16[512,256]{1,0:T(8,128)(2,1)}, u32[]{:S(2)}, u32[]{:S(2)}) collective-permute-start(bf16[512,256]{1,0:T(8,128)(2,1)S(1)} %bitcast_select_fusion.3), channel_id=1, source_target_pairs={{0,7},{1,0},{2,1},{3,2},{4,3},{5,4},{6,5},{7,6},{8,15},{9,8},{10,9... | collective-permute-start | bytes 786440 | tf_op jit(solution)/shard_map/while/body/eval_jaxpr/ppermute | solution.py:11
  105.4 6.9 %collective-permute-start.1 = (bf16[512,256]{1,0:T(8,128)(2,1)}, bf16[512,256]{1,0:T(8,128)(2,1)}, u32[]{:S(2)}, u32[]{:S(2)}) collective-permute-start(bf16[512,256]{1,0:T(8,128)(2,1)} %collective-permute-done), channel_id=1, source_target_pairs={{0,1},{1,2},{2,3},{3,4},{4,5},{5,6},{6,7},{7,0},{8,9},{9,10},{10,1... | collective-permute-start | bytes 786440 | tf_op jit(solution)/shard_map/while/body/eval_jaxpr/ppermute | solution.py:11
  108.3 10.5 %copy-start.4 = (bf16[256,256]{1,0:T(8,128)(2,1)S(1)}, bf16[256,256]{1,0:T(8,128)(2,1)}, u32[]{:S(2)}) copy-start(bf16[256,256]{1,0:T(8,128)(2,1)} %get-tuple-element.604) | copy-start | bytes 393220 | tf_op jit(solution)/shard_map/while
  108.3 9.7 %collective-permute-start.3 = (bf16[512,256]{1,0:T(8,128)(2,1)}, bf16[512,256]{1,0:T(8,128)(2,1)S(1)}, u32[]{:S(2)}, u32[]{:S(2)}) collective-permute-start(bf16[512,256]{1,0:T(8,128)(2,1)} %collective-permute-done.2), channel_id=1, source_target_pairs={{0,7},{1,0},{2,1},{3,2},{4,3},{5,4},{6,5},{7,6},{8,15},{9,8},{10,9... | collective-permute-start | bytes 786440 | tf_op jit(solution)/shard_map/while/body/eval_jaxpr/ppermute | solution.py:11
  123.3 14.4 %collective-permute-start.4 = (bf16[512,256]{0,1:T(8,128)(2,1)S(1)}, bf16[512,256]{0,1:T(8,128)(2,1)}, u32[]{:S(2)}, u32[]{:S(2)}) collective-permute-start(bf16[512,256]{0,1:T(8,128)(2,1)S(1)} %get-tuple-element.550), channel_id=1, source_target_pairs={{0,8},{8,16},{16,24},{1,9},{9,17},{17,25},{2,10},{10,18},{18,26},{... | collective-permute-start | bytes 786440 | tf_op jit(solution)/shard_map/while/body/eval_jaxpr/ppermute | solution.py:25
  137.7 8.4 %copy-start = (bf16[4,512,256]{2,1,0:T(8,128)(2,1)}, bf16[4,512,256]{2,1,0:T(8,128)(2,1)S(1)}, u32[]{:S(2)}) copy-start(bf16[4,512,256]{2,1,0:T(8,128)(2,1)S(1)} %get-tuple-element.573) | copy-start | bytes 3145732 | tf_op jit(solution)/shard_map/while
  139.9 12.1 %collective-permute-start = (bf16[512,256]{1,0:T(8,128)(2,1)S(1)}, bf16[512,256]{1,0:T(8,128)(2,1)}, u32[]{:S(2)}, u32[]{:S(2)}) collective-permute-start(bf16[512,256]{1,0:T(8,128)(2,1)S(1)} %bitcast_select_fusion.3), channel_id=1, source_target_pairs={{0,1},{1,2},{2,3},{3,4},{4,5},{5,6},{6,7},{7,0},{8,9},{9,10},{10,1... | collective-permute-start | bytes 786440 | tf_op jit(solution)/shard_map/while/body/eval_jaxpr/ppermute | solution.py:11
  140.0 14.9 %collective-permute-start.2 = (bf16[512,256]{1,0:T(8,128)(2,1)S(1)}, bf16[512,256]{1,0:T(8,128)(2,1)}, u32[]{:S(2)}, u32[]{:S(2)}) collective-permute-start(bf16[512,256]{1,0:T(8,128)(2,1)S(1)} %bitcast_select_fusion.3), channel_id=1, source_target_pairs={{0,7},{1,0},{2,1},{3,2},{4,3},{5,4},{6,5},{7,6},{8,15},{9,8},{10,9... | collective-permute-start | bytes 786440 | tf_op jit(solution)/shard_map/while/body/eval_jaxpr/ppermute | solution.py:11
  152.1 6.7 %collective-permute-start.1 = (bf16[512,256]{1,0:T(8,128)(2,1)}, bf16[512,256]{1,0:T(8,128)(2,1)}, u32[]{:S(2)}, u32[]{:S(2)}) collective-permute-start(bf16[512,256]{1,0:T(8,128)(2,1)} %collective-permute-done), channel_id=1, source_target_pairs={{0,1},{1,2},{2,3},{3,4},{4,5},{5,6},{6,7},{7,0},{8,9},{9,10},{10,1... | collective-permute-start | bytes 786440 | tf_op jit(solution)/shard_map/while/body/eval_jaxpr/ppermute | solution.py:11
  154.9 10.3 %copy-start.4 = (bf16[256,256]{1,0:T(8,128)(2,1)S(1)}, bf16[256,256]{1,0:T(8,128)(2,1)}, u32[]{:S(2)}) copy-start(bf16[256,256]{1,0:T(8,128)(2,1)} %get-tuple-element.604) | copy-start | bytes 393220 | tf_op jit(solution)/shard_map/while
  154.9 9.6 %collective-permute-start.3 = (bf16[512,256]{1,0:T(8,128)(2,1)}, bf16[512,256]{1,0:T(8,128)(2,1)S(1)}, u32[]{:S(2)}, u32[]{:S(2)}) collective-permute-start(bf16[512,256]{1,0:T(8,128)(2,1)} %collective-permute-done.2), channel_id=1, source_target_pairs={{0,7},{1,0},{2,1},{3,2},{4,3},{5,4},{6,5},{7,6},{8,15},{9,8},{10,9... | collective-permute-start | bytes 786440 | tf_op jit(solution)/shard_map/while/body/eval_jaxpr/ppermute | solution.py:11
  169.8 13.3 %collective-permute-start.4 = (bf16[512,256]{0,1:T(8,128)(2,1)S(1)}, bf16[512,256]{0,1:T(8,128)(2,1)}, u32[]{:S(2)}, u32[]{:S(2)}) collective-permute-start(bf16[512,256]{0,1:T(8,128)(2,1)S(1)} %get-tuple-element.550), channel_id=1, source_target_pairs={{0,8},{8,16},{16,24},{1,9},{9,17},{17,25},{2,10},{10,18},{18,26},{... | collective-permute-start | bytes 786440 | tf_op jit(solution)/shard_map/while/body/eval_jaxpr/ppermute | solution.py:25
  183.1 8.4 %copy-start = (bf16[4,512,256]{2,1,0:T(8,128)(2,1)}, bf16[4,512,256]{2,1,0:T(8,128)(2,1)S(1)}, u32[]{:S(2)}) copy-start(bf16[4,512,256]{2,1,0:T(8,128)(2,1)S(1)} %get-tuple-element.573) | copy-start | bytes 3145732 | tf_op jit(solution)/shard_map/while
  185.3 12.6 %collective-permute-start = (bf16[512,256]{1,0:T(8,128)(2,1)S(1)}, bf16[512,256]{1,0:T(8,128)(2,1)}, u32[]{:S(2)}, u32[]{:S(2)}) collective-permute-start(bf16[512,256]{1,0:T(8,128)(2,1)S(1)} %bitcast_select_fusion.3), channel_id=1, source_target_pairs={{0,1},{1,2},{2,3},{3,4},{4,5},{5,6},{6,7},{7,0},{8,9},{9,10},{10,1... | collective-permute-start | bytes 786440 | tf_op jit(solution)/shard_map/while/body/eval_jaxpr/ppermute | solution.py:11
  185.4 15.4 %collective-permute-start.2 = (bf16[512,256]{1,0:T(8,128)(2,1)S(1)}, bf16[512,256]{1,0:T(8,128)(2,1)}, u32[]{:S(2)}, u32[]{:S(2)}) collective-permute-start(bf16[512,256]{1,0:T(8,128)(2,1)S(1)} %bitcast_select_fusion.3), channel_id=1, source_target_pairs={{0,7},{1,0},{2,1},{3,2},{4,3},{5,4},{6,5},{7,6},{8,15},{9,8},{10,9... | collective-permute-start | bytes 786440 | tf_op jit(solution)/shard_map/while/body/eval_jaxpr/ppermute | solution.py:11
  198.0 6.7 %collective-permute-start.1 = (bf16[512,256]{1,0:T(8,128)(2,1)}, bf16[512,256]{1,0:T(8,128)(2,1)}, u32[]{:S(2)}, u32[]{:S(2)}) collective-permute-start(bf16[512,256]{1,0:T(8,128)(2,1)} %collective-permute-done), channel_id=1, source_target_pairs={{0,1},{1,2},{2,3},{3,4},{4,5},{5,6},{6,7},{7,0},{8,9},{9,10},{10,1... | collective-permute-start | bytes 786440 | tf_op jit(solution)/shard_map/while/body/eval_jaxpr/ppermute | solution.py:11
  200.8 10.3 %copy-start.4 = (bf16[256,256]{1,0:T(8,128)(2,1)S(1)}, bf16[256,256]{1,0:T(8,128)(2,1)}, u32[]{:S(2)}) copy-start(bf16[256,256]{1,0:T(8,128)(2,1)} %get-tuple-element.604) | copy-start | bytes 393220 | tf_op jit(solution)/shard_map/while
  200.8 9.6 %collective-permute-start.3 = (bf16[512,256]{1,0:T(8,128)(2,1)}, bf16[512,256]{1,0:T(8,128)(2,1)S(1)}, u32[]{:S(2)}, u32[]{:S(2)}) collective-permute-start(bf16[512,256]{1,0:T(8,128)(2,1)} %collective-permute-done.2), channel_id=1, source_target_pairs={{0,7},{1,0},{2,1},{3,2},{4,3},{5,4},{6,5},{7,6},{8,15},{9,8},{10,9... | collective-permute-start | bytes 786440 | tf_op jit(solution)/shard_map/while/body/eval_jaxpr/ppermute | solution.py:11
  215.7 12.8 %collective-permute-start.4 = (bf16[512,256]{0,1:T(8,128)(2,1)S(1)}, bf16[512,256]{0,1:T(8,128)(2,1)}, u32[]{:S(2)}, u32[]{:S(2)}) collective-permute-start(bf16[512,256]{0,1:T(8,128)(2,1)S(1)} %get-tuple-element.550), channel_id=1, source_target_pairs={{0,8},{8,16},{16,24},{1,9},{9,17},{17,25},{2,10},{10,18},{18,26},{... | collective-permute-start | bytes 786440 | tf_op jit(solution)/shard_map/while/body/eval_jaxpr/ppermute | solution.py:25
  228.5 8.4 %copy-start = (bf16[4,512,256]{2,1,0:T(8,128)(2,1)}, bf16[4,512,256]{2,1,0:T(8,128)(2,1)S(1)}, u32[]{:S(2)}) copy-start(bf16[4,512,256]{2,1,0:T(8,128)(2,1)S(1)} %get-tuple-element.573) | copy-start | bytes 3145732 | tf_op jit(solution)/shard_map/while
  230.8 13.1 %collective-permute-start = (bf16[512,256]{1,0:T(8,128)(2,1)S(1)}, bf16[512,256]{1,0:T(8,128)(2,1)}, u32[]{:S(2)}, u32[]{:S(2)}) collective-permute-start(bf16[512,256]{1,0:T(8,128)(2,1)S(1)} %bitcast_select_fusion.3), channel_id=1, source_target_pairs={{0,1},{1,2},{2,3},{3,4},{4,5},{5,6},{6,7},{7,0},{8,9},{9,10},{10,1... | collective-permute-start | bytes 786440 | tf_op jit(solution)/shard_map/while/body/eval_jaxpr/ppermute | solution.py:11
  230.8 15.9 %collective-permute-start.2 = (bf16[512,256]{1,0:T(8,128)(2,1)S(1)}, bf16[512,256]{1,0:T(8,128)(2,1)}, u32[]{:S(2)}, u32[]{:S(2)}) collective-permute-start(bf16[512,256]{1,0:T(8,128)(2,1)S(1)} %bitcast_select_fusion.3), channel_id=1, source_target_pairs={{0,7},{1,0},{2,1},{3,2},{4,3},{5,4},{6,5},{7,6},{8,15},{9,8},{10,9... | collective-permute-start | bytes 786440 | tf_op jit(solution)/shard_map/while/body/eval_jaxpr/ppermute | solution.py:11
  243.8 6.7 %collective-permute-start.1 = (bf16[512,256]{1,0:T(8,128)(2,1)}, bf16[512,256]{1,0:T(8,128)(2,1)}, u32[]{:S(2)}, u32[]{:S(2)}) collective-permute-start(bf16[512,256]{1,0:T(8,128)(2,1)} %collective-permute-done), channel_id=1, source_target_pairs={{0,1},{1,2},{2,3},{3,4},{4,5},{5,6},{6,7},{7,0},{8,9},{9,10},{10,1... | collective-permute-start | bytes 786440 | tf_op jit(solution)/shard_map/while/body/eval_jaxpr/ppermute | solution.py:11
  246.7 10.3 %copy-start.4 = (bf16[256,256]{1,0:T(8,128)(2,1)S(1)}, bf16[256,256]{1,0:T(8,128)(2,1)}, u32[]{:S(2)}) copy-start(bf16[256,256]{1,0:T(8,128)(2,1)} %get-tuple-element.604) | copy-start | bytes 393220 | tf_op jit(solution)/shard_map/while
  246.7 9.6 %collective-permute-start.3 = (bf16[512,256]{1,0:T(8,128)(2,1)}, bf16[512,256]{1,0:T(8,128)(2,1)S(1)}, u32[]{:S(2)}, u32[]{:S(2)}) collective-permute-start(bf16[512,256]{1,0:T(8,128)(2,1)} %collective-permute-done.2), channel_id=1, source_target_pairs={{0,7},{1,0},{2,1},{3,2},{4,3},{5,4},{6,5},{7,6},{8,15},{9,8},{10,9... | collective-permute-start | bytes 786440 | tf_op jit(solution)/shard_map/while/body/eval_jaxpr/ppermute | solution.py:11
  261.5 12.4 %collective-permute-start.4 = (bf16[512,256]{0,1:T(8,128)(2,1)S(1)}, bf16[512,256]{0,1:T(8,128)(2,1)}, u32[]{:S(2)}, u32[]{:S(2)}) collective-permute-start(bf16[512,256]{0,1:T(8,128)(2,1)S(1)} %get-tuple-element.550), channel_id=1, source_target_pairs={{0,8},{8,16},{16,24},{1,9},{9,17},{17,25},{2,10},{10,18},{18,26},{... | collective-permute-start | bytes 786440 | tf_op jit(solution)/shard_map/while/body/eval_jaxpr/ppermute | solution.py:25
  276.2 13.5 %collective-permute-start = (bf16[512,256]{1,0:T(8,128)(2,1)S(1)}, bf16[512,256]{1,0:T(8,128)(2,1)}, u32[]{:S(2)}, u32[]{:S(2)}) collective-permute-start(bf16[512,256]{1,0:T(8,128)(2,1)S(1)} %bitcast_select_fusion.3), channel_id=1, source_target_pairs={{0,1},{1,2},{2,3},{3,4},{4,5},{5,6},{6,7},{7,0},{8,9},{9,10},{10,1... | collective-permute-start | bytes 786440 | tf_op jit(solution)/shard_map/while/body/eval_jaxpr/ppermute | solution.py:11
  276.3 16.3 %collective-permute-start.2 = (bf16[512,256]{1,0:T(8,128)(2,1)S(1)}, bf16[512,256]{1,0:T(8,128)(2,1)}, u32[]{:S(2)}, u32[]{:S(2)}) collective-permute-start(bf16[512,256]{1,0:T(8,128)(2,1)S(1)} %bitcast_select_fusion.3), channel_id=1, source_target_pairs={{0,7},{1,0},{2,1},{3,2},{4,3},{5,4},{6,5},{7,6},{8,15},{9,8},{10,9... | collective-permute-start | bytes 786440 | tf_op jit(solution)/shard_map/while/body/eval_jaxpr/ppermute | solution.py:11
  289.7 6.7 %collective-permute-start.1 = (bf16[512,256]{1,0:T(8,128)(2,1)}, bf16[512,256]{1,0:T(8,128)(2,1)}, u32[]{:S(2)}, u32[]{:S(2)}) collective-permute-start(bf16[512,256]{1,0:T(8,128)(2,1)} %collective-permute-done), channel_id=1, source_target_pairs={{0,1},{1,2},{2,3},{3,4},{4,5},{5,6},{6,7},{7,0},{8,9},{9,10},{10,1... | collective-permute-start | bytes 786440 | tf_op jit(solution)/shard_map/while/body/eval_jaxpr/ppermute | solution.py:11
  292.6 10.3 %copy-start.4 = (bf16[256,256]{1,0:T(8,128)(2,1)S(1)}, bf16[256,256]{1,0:T(8,128)(2,1)}, u32[]{:S(2)}) copy-start(bf16[256,256]{1,0:T(8,128)(2,1)} %get-tuple-element.604) | copy-start | bytes 393220 | tf_op jit(solution)/shard_map/while
  292.6 9.6 %collective-permute-start.3 = (bf16[512,256]{1,0:T(8,128)(2,1)}, bf16[512,256]{1,0:T(8,128)(2,1)S(1)}, u32[]{:S(2)}, u32[]{:S(2)}) collective-permute-start(bf16[512,256]{1,0:T(8,128)(2,1)} %collective-permute-done.2), channel_id=1, source_target_pairs={{0,7},{1,0},{2,1},{3,2},{4,3},{5,4},{6,5},{7,6},{8,15},{9,8},{10,9... | collective-permute-start | bytes 786440 | tf_op jit(solution)/shard_map/while/body/eval_jaxpr/ppermute | solution.py:11
  307.4 11.9 %collective-permute-start.4 = (bf16[512,256]{0,1:T(8,128)(2,1)S(1)}, bf16[512,256]{0,1:T(8,128)(2,1)}, u32[]{:S(2)}, u32[]{:S(2)}) collective-permute-start(bf16[512,256]{0,1:T(8,128)(2,1)S(1)} %get-tuple-element.550), channel_id=1, source_target_pairs={{0,8},{8,16},{16,24},{1,9},{9,17},{17,25},{2,10},{10,18},{18,26},{... | collective-permute-start | bytes 786440 | tf_op jit(solution)/shard_map/while/body/eval_jaxpr/ppermute | solution.py:25
  (11 other events, 34.4 us)
where the time goes:
time: 323 us; the launch traced here: 320 us
  waiting for transfers between devices  119 us (37%)
  local copies, waits for them, and re-layouts  83.1 us (26%)
  matrix products  45.2 us (14%)
  starting transfers between devices  42.1 us (13%)
  other arithmetic  29.8 us (9%)
    ppermute x7, waiting for transfers between devices, passed_along(): return lax.ppermute(x, axis, pairs)  66.5 us
    ppermute x28, waiting for transfers between devices, from_behind(): return lax.ppermute(x, axis, [(i, (i + by) % peers) for i in range(peers)])  52.7 us
    while x77, local copies, waits for them, and re-layouts  45.1 us
    ppermute x28, starting transfers between devices, from_behind(): return lax.ppermute(x, axis, [(i, (i + by) % peers) for i in range(peers)])  28.7 us
    dot_general x7, matrix products, node_layer(): jnp.dot(neighbour_mean, neighbour_matrix, preferred_element_type=jnp.floa...  23.4 us
    dynamic_slice x7, local copies, waits for them, and re-layouts, node_layer(): values = lax.dynamic_index_in_dim(tile_values, batch, 0, keepdims=False)  14.4 us
    dot_general x7, matrix products, aggregate(): jnp.dot(placing, values.reshape(slot_total, block_size * block_size), pre...  14.3 us
    ppermute x7, starting transfers between devices, passed_along(): return lax.ppermute(x, axis, pairs)  13.5 us
  transfers between devices with their start and end apart: 35, of which 21 were waited for; matrix products, arithmetic and copies ran while one was open for 32% of the time, Pallas kernels for 0%

commit v1 on v0

v1 whole, which is shorter than its diff:
```python
import functools

import jax
import jax.numpy as jnp
from jax import lax
from jax.experimental import pallas as pl
from jax.experimental.pallas import tpu as pltpu
from jax.sharding import PartitionSpec as P

REACH = 2
SPAN = 2 * REACH + 1
MESH = pl.DeviceIdType.MESH


def kernel(
    sections, peers, batches, blocks, chunks,
    slot_ref, deg_ref, feat_ref, vals_ref, ws_ref, wn_ref, out_ref,
    tiles, slab, win, wbuf, acc, own_part, rdeg,
    local_sem, send_sem, recv_sem, fwd_sem, wsend_sem, wrecv_sem, osend_sem, orecv_sem,
):
    section = lax.axis_index("section")
    me = lax.axis_index("blk")
    group = sections // batches
    batch = section // group
    odd = lax.rem(me, 2)
    peer = me + 1 - 2 * odd
    up = lax.rem(me + 2, peers)
    down = lax.rem(me + peers - 2, peers)
    slots = vals_ref.shape[1]
    block = vals_ref.shape[2]
    rows_dev = feat_ref.shape[1]
    size = rows_dev // chunks
    layers = sections
    pslot = 3 - 2 * odd
    fsrc = 4 - 4 * odd
    fdst = 3 - 2 * odd
    other = 4 * odd
    fslot = 1 + 2 * odd

    own_copy = pltpu.make_async_copy(feat_ref.at[batch], win.at[0, REACH], local_sem.at[0])
    own_copy.start()
    vals_copy = pltpu.make_async_copy(
        vals_ref.at[batch], tiles.at[pl.ds(0, slots)], local_sem.at[1]
    )
    vals_copy.start()
    w_copies = [
        pltpu.make_async_copy(ref.at[0], wbuf.at[section, i], local_sem.at[2 + i])
        for i, ref in enumerate((ws_ref, wn_ref))
    ]
    for copy in w_copies:
        copy.start()

    barrier = pltpu.get_barrier_semaphore()
    for near in (peer, up, down):
        pl.semaphore_signal(barrier, inc=1, device_id=(section, near), device_id_type=MESH)
    for k in range(1, sections):
        pl.semaphore_signal(
            barrier, inc=1, device_id=(lax.rem(section + k, sections), me), device_id_type=MESH
        )
    pl.semaphore_wait(barrier, 3 + sections - 1)

    def halo(par, c, way):
        rows = pl.ds(c * size, size)
        target, slot = ((up, 0), (down, 4), (peer, 1 + 2 * odd))[way]
        return pltpu.make_async_remote_copy(
            src_ref=win.at[par, REACH, rows],
            dst_ref=win.at[par, slot, rows],
            send_sem=send_sem.at[way, c],
            recv_sem=recv_sem.at[par, slot, c],
            device_id=(section, target),
            device_id_type=MESH,
        )

    def forward(par, c):
        rows = pl.ds(c * size, size)
        return pltpu.make_async_remote_copy(
            src_ref=win.at[par, fsrc, rows],
            dst_ref=win.at[par, fdst, rows],
            send_sem=fwd_sem.at[c],
            recv_sem=recv_sem.at[par, fdst, c],
            device_id=(section, peer),
            device_id_type=MESH,
        )

    def arrival(par, slot, c):
        rows = pl.ds(c * size, size)
        return pltpu.make_async_remote_copy(
            src_ref=win.at[par, slot, rows],
            dst_ref=win.at[par, slot, rows],
            send_sem=fwd_sem.at[c],
            recv_sem=recv_sem.at[par, slot, c],
            device_id=(section, peer),
            device_id_type=MESH,
        )

    def weight(k, i):
        ref = (ws_ref, wn_ref)[i]
        return pltpu.make_async_remote_copy(
            src_ref=ref.at[0],
            dst_ref=wbuf.at[section, i],
            send_sem=wsend_sem.at[k, i],
            recv_sem=wrecv_sem.at[section, i],
            device_id=(lax.rem(section + k, sections), me),
            device_id_type=MESH,
        )

    def weight_arrival(layer, i):
        return pltpu.make_async_remote_copy(
            src_ref=wbuf.at[layer, i],
            dst_ref=wbuf.at[layer, i],
            send_sem=wsend_sem.at[0, i],
            recv_sem=wrecv_sem.at[layer, i],
            device_id=(lax.rem(section + 1, sections), me),
            device_id_type=MESH,
        )

    def output_local(par, c):
        rows = pl.ds(c * size, size)
        return pltpu.make_async_copy(
            win.at[par, REACH, rows], out_ref.at[0, batch, rows], osend_sem.at[c]
        )

    def output_remote(layer, par, c):
        rows = pl.ds(c * size, size)
        return pltpu.make_async_remote_copy(
            src_ref=win.at[par, REACH, rows],
            dst_ref=out_ref.at[0, batch, rows],
            send_sem=osend_sem.at[c],
            recv_sem=orecv_sem.at[batch, c],
            device_id=(layer, me),
            device_id_type=MESH,
        )

    def output_arrival(m, c):
        rows = pl.ds(c * size, size)
        return pltpu.make_async_remote_copy(
            src_ref=win.at[0, REACH, rows],
            dst_ref=out_ref.at[0, m, rows],
            send_sem=osend_sem.at[c],
            recv_sem=orecv_sem.at[m, c],
            device_id=(lax.rem(section + 1, sections), me),
            device_id_type=MESH,
        )

    def is_sender(layer):
        return jnp.logical_and(
            layer != section, lax.rem(layer, group) == lax.rem(section, group)
        )

    own_copy.wait()
    for c in range(chunks):
        for way in range(3):
            halo(0, c, way).start()
    for k in range(1, sections):
        for i in range(2):
            weight(k, i).start()

    tiles[slots] = jnp.zeros((block, block), tiles.dtype)
    for r in range(blocks):
        span = pl.ds(r * block, block)
        degrees = deg_ref[:, span].astype(jnp.float32)
        chosen = lax.broadcasted_iota(jnp.int32, degrees.shape, 0) == batch
        degree = jnp.sum(jnp.where(chosen, degrees, 0.0), axis=0, keepdims=True)
        column = jnp.broadcast_to(1.0 / degree, (block, block)).T
        for half in range(rdeg.shape[1] // block):
            rdeg[span, pl.ds(half * block, block)] = column
    for copy in w_copies:
        copy.wait()
    vals_copy.wait()

    def place(s, carry):
        for r in range(blocks):
            for c in range(blocks):
                slot = slot_ref[batch, r * (SPAN * blocks) + s * blocks + c]
                slab[s, r * block:(r + 1) * block, c * block:(c + 1) * block] = tiles[slot]
        return carry

    lax.fori_loop(0, SPAN, place, 0)

    def dot(a, b):
        return jnp.dot(a, b, preferred_element_type=jnp.float32)

    def layer_step(layer, carry):
        par = lax.rem(layer, 2)
        nxt = 1 - par

        @pl.when(layer != section)
        def _():
            for i in range(2):
                weight_arrival(layer, i).wait_recv()

        own_part[...] = dot(win[par, REACH], wbuf[layer, 0])
        acc[...] = dot(slab[REACH], win[par, REACH])
        for c in range(chunks):
            arrival(par, fsrc, c).wait_recv()
            forward(par, c).start()
        for c in range(chunks):
            arrival(par, pslot, c).wait_recv()
        acc[...] += dot(slab[pslot], win[par, pslot])
        acc[...] += dot(slab[fsrc], win[par, fsrc])
        for c in range(chunks):
            arrival(par, other, c).wait_recv()
        acc[...] += dot(slab[other], win[par, other])
        for c in range(chunks):
            arrival(par, fslot, c).wait_recv()
        acc[...] += dot(slab[fslot], win[par, fslot])

        for c in range(chunks):
            for way in range(3):
                halo(par, c, way).wait_send()
            forward(par, c).wait_send()

        @pl.when(layer - 1 == section)
        def _():
            for c in range(chunks):
                output_local(par, c).wait()

        @pl.when(jnp.logical_and(layer >= 1, is_sender(layer - 1)))
        def _():
            for c in range(chunks):
                output_remote(layer - 1, par, c).wait_send()

        for c in range(chunks):
            rows = pl.ds(c * size, size)
            mean = (acc[rows, :] * rdeg[rows, :]).astype(jnp.bfloat16)
            combined = own_part[rows, :] + dot(mean, wbuf[layer, 1])
            active = jnp.maximum(combined, 0.0)
            scale = lax.rsqrt(jnp.mean(active * active, axis=-1, keepdims=True) + 1e-05)
            win[nxt, REACH, rows, :] = (active * scale).astype(jnp.bfloat16)

            @pl.when(layer < layers - 1)
            def _():
                for way in range(3):
                    halo(nxt, c, way).start()

            @pl.when(layer == section)
            def _():
                output_local(nxt, c).start()

            @pl.when(is_sender(layer))
            def _():
                output_remote(layer, nxt, c).start()

        return carry

    lax.fori_loop(0, layers, layer_step, 0)

    last = layers - 1

    @pl.when(section == last)
    def _():
        for c in range(chunks):
            output_local(layers % 2, c).wait()

    @pl.when(is_sender(last))
    def _():
        for c in range(chunks):
            output_remote(last, layers % 2, c).wait_send()

    for m in range(batches):

        @pl.when(batch != m)
        def _():
            for c in range(chunks):
                output_arrival(m, c).wait_recv()

    for k in range(1, sections):
        for i in range(2):
            weight(k, i).wait_send()


def slot_table(tile_rows, tile_cols, tile_count, blocks_dev, blk_count):
    slot_total = tile_rows.shape[1]
    band = SPAN * blocks_dev
    blk_index = lax.axis_index("blk")
    shifted = jnp.mod(tile_cols // blocks_dev - blk_index + REACH, blk_count)
    column_local = shifted * blocks_dev + jnp.mod(tile_cols, blocks_dev)
    row_local = tile_rows - blk_index * blocks_dev
    target = row_local * band + column_local
    ids = jnp.arange(slot_total, dtype=jnp.int32)
    target = jnp.where(ids[None, :] < tile_count, target, -1)
    places = jnp.arange(blocks_dev * band, dtype=jnp.int32)
    hit = target[:, None, :] == places[None, :, None]
    return jnp.min(jnp.where(hit, ids[None, None, :], slot_total), axis=2)


def body(
    features, tile_values, tile_rows, tile_cols, tile_count, degrees, self_weight, neighbour_weight
):
    batches, rows_dev, width = features.shape
    slots, block = tile_values.shape[1], tile_values.shape[2]
    blocks = rows_dev // block
    sections = lax.axis_size("section")
    peers = lax.axis_size("blk")
    chunks = blocks
    table = slot_table(tile_rows, tile_cols, tile_count, blocks, peers)
    anywhere = pl.BlockSpec(memory_space=pl.ANY)
    hbm = pl.BlockSpec(memory_space=pltpu.HBM)
    dma = pltpu.SemaphoreType.DMA
    return pl.pallas_call(
        functools.partial(kernel, sections, peers, batches, blocks, chunks),
        out_shape=jax.ShapeDtypeStruct((1, batches, rows_dev, width), jnp.bfloat16),
        in_specs=[
            pl.BlockSpec(memory_space=pltpu.SMEM),
            pl.BlockSpec(memory_space=pltpu.VMEM),
            hbm, hbm, hbm, hbm,
        ],
        out_specs=anywhere,
        scratch_shapes=[
            pltpu.VMEM((slots + 1, block, block), jnp.bfloat16),
            pltpu.VMEM((SPAN, rows_dev, rows_dev), jnp.bfloat16),
            pltpu.VMEM((2, SPAN, rows_dev, width), jnp.bfloat16),
            pltpu.VMEM((sections, 2, width, width), jnp.bfloat16),
            pltpu.VMEM((rows_dev, width), jnp.float32),
            pltpu.VMEM((rows_dev, width), jnp.float32),
            pltpu.VMEM((rows_dev, width), jnp.float32),
            dma((4,)),
            dma((3, chunks)),
            dma((2, SPAN, chunks)),
            dma((chunks,)),
            dma((sections, 2)),
            dma((sections, 2)),
            dma((chunks,)),
            dma((batches, chunks)),
        ],
        compiler_params=pltpu.CompilerParams(
            collective_id=0, has_side_effects=True, vmem_limit_bytes=40 * 1024 * 1024
        ),
    )(table, degrees, features, tile_values, self_weight, neighbour_weight)


def solution(mesh):
    return jax.shard_map(
        body,
        mesh=mesh,
        in_specs=(
            P(None, "blk", None),
            P(None, "blk", None, None),
            P(None, "blk"),
            P(None, "blk"),
            P(None, "blk"),
            P(None, "blk"),
            P("section", None, None),
            P("section", None, None),
        ),
        out_specs=P("section", None, "blk", None),
        check_vma=False,
    )
```

time: 323 us -> 87.4 us (0.27)
  the two profiles are of different devices: /device:TPU:22 before, /device:TPU:3 now
where the time goes in v1:
time: 87.4 us; the launch traced here: 87.1 us
  Pallas kernels  77.5 us (89%)
  local copies, waits for them, and re-layouts  8.7 us (10%)
  other arithmetic  0.92 us (1%)
    pallas_call x1, Pallas kernels, body(): pl.pallas_call(functools.partial(kernel, sections, peers, batches, blocks...  77.5 us
    unnamed x11, local copies, waits for them, and re-layouts  8.7 us

profile of v1, /device:TPU:3, one launch (start us, length us, event | category | flops | bytes accessed | tf_op | source)
XLA Modules:
  0.0 87.1 jit_solution(2354930195070305255)
XLA Ops:
  0.0 0.8 fusion.6
  0.8 0.1 select_reduce_fusion.slot_ref
  0.9 0.0 copy-start
  0.9 4.0 %copy-done = bf16[4,80,128,128]{3,2,1,0:T(8,128)(2,1)S(1)} copy-done((bf16[4,80,128,128]{3,2,1,0:T(8,128)(2,1)S(1)}, bf16[4,80,128,128]{3,2,1,0:T(8,128)(2,1)}, u32[]{:S(2)}) %copy-start) | copy-done | bytes 10485784
  4.9 0.0 copy-start.1
  4.9 1.2 %copy-done.1 = bf16[4,512,256]{2,1,0:T(8,128)(2,1)S(1)} copy-done((bf16[4,512,256]{2,1,0:T(8,128)(2,1)S(1)}, bf16[4,512,256]{2,1,0:T(8,128)(2,1)}, u32[]{:S(2)}) %copy-start.1) | copy-done | bytes 1048600
  6.1 0.0 copy-start.2
  6.2 0.9 %copy-done.2 = bf16[1,256,256]{2,1,0:T(8,128)(2,1)S(1)} copy-done((bf16[1,256,256]{2,1,0:T(8,128)(2,1)S(1)}, bf16[1,256,256]{2,1,0:T(8,128)(2,1)}, u32[]{:S(2)}) %copy-start.2) | copy-done | bytes 131096
  7.1 0.0 copy-start.3
  7.1 0.9 %copy-done.3 = bf16[1,256,256]{2,1,0:T(8,128)(2,1)S(1)} copy-done((bf16[1,256,256]{2,1,0:T(8,128)(2,1)S(1)}, bf16[1,256,256]{2,1,0:T(8,128)(2,1)}, u32[]{:S(2)}) %copy-start.3) | copy-done | bytes 131096
  8.0 0.0 copy-start.4
  8.0 0.7 copy-done.4
  8.7 77.5 %shard_map.82 = bf16[1,4,512,256]{3,2,1,0:T(8,128)(2,1)S(1)} custom-call(s32[4,80]{1,0:T(4,128)S(1)} %select_reduce_fusion.slot_ref, s32[4,512]{1,0:T(4,128)S(1)} %copy-done.4, bf16[4,512,256]{2,1,0:T(8,128)(2,1)S(1)} %copy-done.1, bf16[4,80,128,128]{3,2,1,0:T(8,128)(2,1)S(1)} %copy-done, bf16[1,256,256]{2,1,0:T(8,128)(2,1)S(1)} %copy-done.2, ...), custom_call_target="tpu_custom_call" | custom-call | tf_op jit(solution)/shard_map/pallas_call | solution.py:300
  86.1 1.0 %copy.10 = bf16[1,4,512,256]{3,2,1,0:T(8,128)(2,1)} copy(bf16[1,4,512,256]{3,2,1,0:T(8,128)(2,1)S(1)} %shard_map.82) | data formatting | bytes 2097152
Async XLA Ops:
  0.9 4.0 %copy-start = (bf16[4,80,128,128]{3,2,1,0:T(8,128)(2,1)S(1)}, bf16[4,80,128,128]{3,2,1,0:T(8,128)(2,1)}, u32[]{:S(2)}) copy-start(bf16[4,80,128,128]{3,2,1,0:T(8,128)(2,1)} %vals_ref.1) | copy-start | bytes 31457284
  4.9 1.2 %copy-start.1 = (bf16[4,512,256]{2,1,0:T(8,128)(2,1)S(1)}, bf16[4,512,256]{2,1,0:T(8,128)(2,1)}, u32[]{:S(2)}) copy-start(bf16[4,512,256]{2,1,0:T(8,128)(2,1)} %feat_ref.1) | copy-start | bytes 3145732
  6.1 0.9 %copy-start.2 = (bf16[1,256,256]{2,1,0:T(8,128)(2,1)S(1)}, bf16[1,256,256]{2,1,0:T(8,128)(2,1)}, u32[]{:S(2)}) copy-start(bf16[1,256,256]{2,1,0:T(8,128)(2,1)} %ws_ref.1) | copy-start | bytes 393220
  7.1 0.9 %copy-start.3 = (bf16[1,256,256]{2,1,0:T(8,128)(2,1)S(1)}, bf16[1,256,256]{2,1,0:T(8,128)(2,1)}, u32[]{:S(2)}) copy-start(bf16[1,256,256]{2,1,0:T(8,128)(2,1)} %wn_ref.1) | copy-start | bytes 393220
  8.0 0.7 copy-start.4

commit v2 on v1

--- a/solution.py
+++ b/solution.py
@@ -16,12 +16,13 @@
     sections, peers, batches, blocks, chunks,
     slot_ref, deg_ref, feat_ref, vals_ref, ws_ref, wn_ref, out_ref,
     tiles, slab, win, wbuf, acc, own_part, rdeg,
-    local_sem, send_sem, recv_sem, fwd_sem, wsend_sem, wrecv_sem, osend_sem, orecv_sem,
+    local_sem, send_sem, recv_sem, fwd_sem, wsend_sem, wrecv_sem, osend_sem, orecv_sem, turn_sem,
 ):
     section = lax.axis_index("section")
     me = lax.axis_index("blk")
     group = sections // batches
     batch = section // group
+    late = lax.rem(section, 2)
     odd = lax.rem(me, 2)
     peer = me + 1 - 2 * odd
     up = lax.rem(me + 2, peers)
@@ -148,9 +149,13 @@
         )
 
     own_copy.wait()
-    for c in range(chunks):
-        for way in range(3):
-            halo(0, c, way).start()
+
+    @pl.when(late == 0)
+    def _():
+        for c in range(chunks):
+            for way in range(3):
+                halo(0, c, way).start()
+
     for k in range(1, sections):
         for i in range(2):
             weight(k, i).start()
@@ -177,6 +182,13 @@
 
     lax.fori_loop(0, SPAN, place, 0)
 
+    @pl.when(late == 1)
+    def _():
+        pl.semaphore_wait(turn_sem, 1)
+        for c in range(chunks):
+            for way in range(3):
+                halo(0, c, way).start()
+
     def dot(a, b):
         return jnp.dot(a, b, preferred_element_type=jnp.float32)
 
@@ -200,6 +212,13 @@
         acc[...] += dot(slab[fsrc], win[par, fsrc])
         for c in range(chunks):
             arrival(par, other, c).wait_recv()
+
+        @pl.when(jnp.logical_and(layer == 0, late == 0))
+        def _():
+            pl.semaphore_signal(
+                turn_sem, inc=1, device_id=(section + 1, me), device_id_type=MESH
+            )
+
         acc[...] += dot(slab[other], win[par, other])
         for c in range(chunks):
             arrival(par, fslot, c).wait_recv()
@@ -322,9 +341,10 @@
             dma((sections, 2)),
             dma((chunks,)),
             dma((batches, chunks)),
+            pltpu.SemaphoreType.REGULAR,
         ],
         compiler_params=pltpu.CompilerParams(
-            collective_id=0, has_side_effects=True, vmem_limit_bytes=40 * 1024 * 1024
+            collective_id=0, has_side_effects=True, vmem_limit_bytes=60 * 1024 * 1024
         ),
     )(table, degrees, features, tile_values, self_weight, neighbour_weight)
 

time: 87.4 us -> 73.7 us (0.84)
  Pallas kernels: 77.5 us -> 69.7 us
  local copies, waits for them, and re-layouts: 8.7 us -> 2.26 us
    pallas_call x1, Pallas kernels: 77.5 us -> 69.7 us  [body(): pl.pallas_call(functools.partial(kernel, sections, peers, batches, blocks...]
    unnamed x11 -> x1, local copies, waits for them, and re-layouts: 8.7 us -> 2.26 us
where the time goes in v2:
time: 73.7 us; the launch traced here: 73.5 us
  Pallas kernels  69.7 us (95%)
  local copies, waits for them, and re-layouts  2.26 us (3%)
  other arithmetic  1.5 us (2%)
    pallas_call x1, Pallas kernels, body(): pl.pallas_call(functools.partial(kernel, sections, peers, batches, blocks...  69.7 us
    unnamed x1, local copies, waits for them, and re-layouts  2.26 us

profile of v2, /device:TPU:3, one launch (start us, length us, event | category | flops | bytes accessed | tf_op | source)
XLA Modules:
  0.0 73.5 jit_solution(5567245326297002170)
XLA Ops:
  0.0 0.8 %fusion.6 = s32[4,80]{1,0:T(4,128)S(1)} fusion(s32[4,80]{1,0:T(4,128)} %param.10, s32[4,80]{1,0:T(4,128)} %param.11, s32[]{:T(128)S(6)} %axis_index.12, s32[]{:T(128)S(6)} %mul.13, s32[4]{0:T(128)} %bitcast.1), kind=kLoop, calls=%fused_computation.16 | loop fusion | flops 12480 | bytes 3864 | tf_op jit(solution)/shard_map/jit(_where)/select_n | solution.py:300
  0.8 0.7 select_reduce_fusion.slot_ref
  1.5 69.7 %shard_map.82 = bf16[1,4,512,256]{3,2,1,0:T(8,128)(2,1)} custom-call(s32[4,80]{1,0:T(4,128)} %select_reduce_fusion.slot_ref, s32[4,512]{1,0:T(4,128)} %deg_ref.1, bf16[4,512,256]{2,1,0:T(8,128)(2,1)} %feat_ref.1, bf16[4,80,128,128]{3,2,1,0:T(8,128)(2,1)} %vals_ref.1, bf16[1,256,256]{2,1,0:T(8,128)(2,1)} %ws_ref.1, bf16[1,256,256]{2,1,0:T(8,128)(2,1)} %wn_ref.1), custom_call_target="tpu_custom_call" | custom-call | tf_op jit(solution)/shard_map/pallas_call | solution.py:319
  71.2 2.3 %copy.10 = bf16[1,4,512,256]{3,2,1,0:T(8,128)(2,1)} copy(bf16[1,4,512,256]{3,2,1,0:T(8,128)(2,1)} %shard_map.82) | data formatting | bytes 2097152
